TPU v7x, 512 devices: a whole 4x4x16 slice. The times are simulated.
512 devices in a mesh: seq: 64 (over z, y), tp: 8 (over x, core).
Axes of the slice: x: 4, y: 4, z: 16, core: 2. Of those that a mesh axis runs over, the one named last changes fastest.
Arguments:
- byte_states: bfloat16 [40960, 1024], P('seq')
- patch_starts: int32 [8960], P('seq'), may hold values from 0 to 640, as said below
- query_weight: bfloat16 [1024, 1024], P(None, 'tp'), may hold values from -0.1875 to 0.1875
- key_weight: bfloat16 [1024, 1024], P(None, 'tp'), may hold values from -0.1875 to 0.1875
- value_weight: bfloat16 [1024, 1024], P(None, 'tp'), may hold values from -0.1875 to 0.1875
- out_weight: bfloat16 [1024, 1024], P('tp'), may hold values from -0.1875 to 0.1875
- up_weight: bfloat16 [1024, 4096], P(None, 'tp'), may hold values from -0.09375 to 0.09375
- patch_grad: bfloat16 [5120, 4096], P('seq', 'tp'), may hold values from -6 to 6
- owner_slots: int32 [64], replicated, may hold values from 0 to 63, each once
Outputs:
- byte_grad: bfloat16 [40960, 1024], P('seq', 'tp')
- owned_grads: float32 [4096, 1024], P('seq', 'tp')
Inputs may be any that keep to these rules, and one draw needn't show every extreme that they name: `patch_starts`: each device's 140 slots list in ascending order the offsets at which patches begin in its bytes, then 640 in unused slots. Byte 0 of the first device begins a patch. Every device's first patch begins before offset 128, and on some device at offset 128 - 1. Devices 2i and 2i + 1 together hold 160 patch starts; every device holds at least 20 and at most 140, and some device holds exactly 140. Device 0 holds more than 80.
All inputs are finite; a program needn't handle non-finite values.
Results may differ from a plain program's by a relative error of at most 0.04.
Values may be sent and summed in bfloat16 or wider, within the bound.
A program may use at most 64 MiB of HBM per device.

v0:
```python
import jax
import jax.numpy as jnp
from jax import lax
from jax.sharding import PartitionSpec as P

HEAD = 64
TAIL = 128


NEG_FLOOR = -1e30
HIGHEST = lax.Precision.HIGHEST
CONTRACT_ROWS = (((0,), (0,)), ((), ()))


def shortened(value):

    def short(part):
        return part.astype(jnp.bfloat16) if part.dtype == jnp.float32 else part

    return jax.tree.map(short, value)


def passed_along(block, axis, distance):
    devices = range(lax.axis_size(axis))
    route = [(i - distance, i) for i in devices if i - distance in devices]
    return lax.ppermute(block, axis, route)


def partner_2(value, axis, bit):
    return lax.ppermute(value, axis, [(i, i ^ 1 << bit) for i in range(lax.axis_size(axis))])


def neighbour(payload, offset):
    return jax.tree.map(
        lambda part, own: part.astype(own.dtype),
        passed_along(shortened(payload), "seq", offset),
        payload,
    )


def to_owner(block, partner, parity, owned):
    even_buffer = jnp.concatenate([block, partner], axis=0)
    odd_buffer = jnp.concatenate([partner, block], axis=0)
    buffer = jnp.where(parity == 0, even_buffer, odd_buffer)
    slot_count = buffer.shape[0]
    offset = jnp.where(parity == 0, 0, slot_count - owned)
    rolled = jnp.roll(buffer, -offset, axis=0)
    keep = jnp.arange(slot_count) < owned
    return jnp.where(keep[:, None], rolled, jnp.zeros_like(rolled))


def local(
    byte_states,
    patch_starts,
    query_weight,
    key_weight,
    value_weight,
    out_weight,
    up_weight,
    patch_grad,
    owner_slots,
):
    fp = jnp.float32
    bf = jnp.bfloat16
    byte_dev = byte_states.shape[0]
    width = byte_states.shape[1]
    slot_count = patch_starts.shape[0]
    rows_dev = patch_grad.shape[0]
    margin = slot_count - rows_dev
    tail_len = TAIL
    columns = query_weight.shape[1]
    heads_here = columns // HEAD
    scale = HEAD ** (-0.5)
    parity = lax.axis_index("seq") % 2
    owned = jnp.sum((patch_starts < byte_dev).astype(jnp.int32))
    first_start = patch_starts[0]
    own_tail = jnp.arange(tail_len) < first_start
    tail_rows, tail_mask = neighbour((byte_states[:tail_len], own_tail.astype(bf)), -1)
    extended = jnp.concatenate([byte_states, tail_rows], axis=0)
    positions = jnp.arange(byte_dev)
    local_segment = (
        jnp.sum((patch_starts[None, :] <= positions[:, None]).astype(jnp.int32), axis=1) - 1
    )
    tail_segment = jnp.where(tail_mask > 0, owned - 1, -1)
    segment_of = jnp.concatenate([local_segment, tail_segment])
    live = segment_of >= 0
    segment_safe = jnp.maximum(segment_of, 0)
    member = segment_of[None, :] == jnp.arange(slot_count)[:, None]
    member_f = member.astype(fp)
    counts = jnp.sum(member_f, axis=1)
    counts_safe = jnp.maximum(counts, 1.0)
    pooled_sum = jnp.dot(member.astype(bf), extended, preferred_element_type=fp)
    pooled = (pooled_sum / counts_safe[:, None]).astype(bf)
    queries = jnp.dot(pooled, query_weight, preferred_element_type=fp).astype(bf)
    key_rows = jnp.dot(extended, key_weight, preferred_element_type=fp).astype(bf)
    value_rows = jnp.dot(extended, value_weight, preferred_element_type=fp).astype(bf)
    query_bytes = jnp.take(queries, segment_safe, axis=0).astype(fp)
    scores = (query_bytes * key_rows.astype(fp)).reshape(-1, heads_here, HEAD).sum(-1) * scale
    masked = jnp.where(member[:, :, None], scores[None, :, :], NEG_FLOOR)
    patch_max = jnp.max(masked, axis=1)
    shifted = scores - jnp.take(patch_max, segment_safe, axis=0)
    expo = jnp.where(live[:, None], jnp.exp(jnp.minimum(shifted, 0.0)), 0.0)
    denom = jnp.dot(member_f, expo, precision=HIGHEST)
    weights = expo / jnp.take(denom, segment_safe, axis=0)
    weights_bf = lax.optimization_barrier(weights.astype(bf))
    weights_wide = jnp.repeat(weights_bf.astype(fp), HEAD, axis=1)
    attended = jnp.dot(member_f, weights_wide * value_rows.astype(fp), precision=HIGHEST).astype(bf)
    send_start = jnp.where(parity == 0, rows_dev - margin, 0)
    window = lax.dynamic_slice_in_dim(patch_grad, send_start, margin, 0)
    partner = partner_2(window, "seq", 0)
    owner_rows = to_owner(patch_grad, partner, parity, owned)
    grad_mix = lax.psum(jnp.dot(owner_rows, up_weight.T, preferred_element_type=fp), "tp")
    mix_bf = grad_mix.astype(bf)
    grad_attended = jnp.dot(mix_bf, out_weight.T, preferred_element_type=fp).astype(bf)
    out_grad_t = lax.dot_general(mix_bf, attended, CONTRACT_ROWS, preferred_element_type=fp)
    delta = (
        (grad_attended.astype(fp) * attended.astype(fp))
        .reshape(slot_count, heads_here, HEAD)
        .sum(-1)
    )
    grad_bytes = jnp.take(grad_attended, segment_safe, axis=0).astype(fp)
    grad_weights = (grad_bytes * value_rows.astype(fp)).reshape(-1, heads_here, HEAD).sum(-1)
    grad_scores = weights * (grad_weights - jnp.take(delta, segment_safe, axis=0))
    grad_values = (weights_wide * grad_bytes).astype(bf)
    score_wide = jnp.repeat(grad_scores, HEAD, axis=1)
    grad_keys = (score_wide * query_bytes * scale).astype(bf)
    grad_queries = (
        jnp.dot(member_f, score_wide * key_rows.astype(fp), precision=HIGHEST) * scale
    ).astype(bf)
    key_grad = lax.dot_general(extended, grad_keys, CONTRACT_ROWS, preferred_element_type=fp)
    value_grad = lax.dot_general(extended, grad_values, CONTRACT_ROWS, preferred_element_type=fp)
    query_grad = lax.dot_general(pooled, grad_queries, CONTRACT_ROWS, preferred_element_type=fp)
    pooled_back = (
        jnp.dot(grad_queries, query_weight.T, preferred_element_type=fp) / counts_safe[:, None]
    )
    partial_value = jnp.dot(grad_keys, key_weight.T, preferred_element_type=fp)
    partial_value = partial_value + jnp.dot(grad_values, value_weight.T, preferred_element_type=fp)
    partial_value = partial_value + jnp.where(
        live[:, None], jnp.take(pooled_back, segment_safe, axis=0), 0.0
    )
    summed = lax.psum_scatter(
        partial_value.astype(jnp.bfloat16), "tp", scatter_dimension=1, tiled=True
    ).astype(jnp.float32)
    out_cols = width // lax.axis_size("tp")
    mix_cols = (
        lax.dynamic_slice_in_dim(grad_mix, lax.axis_index("tp") * out_cols, out_cols, 1)
        / counts_safe[:, None]
    )
    pooled_term = jnp.where(live[:, None], jnp.take(mix_cols, segment_safe, axis=0), 0.0)
    combined = (summed + pooled_term).astype(bf)
    back_rows = neighbour(combined[byte_dev:], 1)
    head_rows = jnp.where(own_tail[:, None], back_rows, combined[:tail_len])
    byte_grad = jnp.concatenate([head_rows, combined[tail_len:byte_dev]], axis=0)
    stacked = jnp.stack([query_grad, key_grad, value_grad, out_grad_t])
    grad_blocks = stacked.reshape(owner_slots.shape[0], -1, columns)
    ordered = jnp.take(grad_blocks, owner_slots, axis=0).reshape(-1, columns)
    owned_grads = lax.psum_scatter(ordered, "seq", scatter_dimension=0, tiled=True)
    return (byte_grad, owned_grads)


def solution(mesh):
    in_specs = (
        P("seq", None),
        P("seq"),
        P(None, "tp"),
        P(None, "tp"),
        P(None, "tp"),
        P("tp", None),
        P(None, "tp"),
        P("seq", "tp"),
        P(),
    )
    out_specs = (P("seq", "tp"), P("seq", "tp"))
    return jax.shard_map(local, mesh=mesh, in_specs=in_specs, out_specs=out_specs, check_vma=False)
```

profile of v0, /device:TPU:6, one launch (start us, length us, event | category | flops | bytes accessed | tf_op | source)
XLA Modules:
  0.0 891.1 jit_solution(11805760125681909715)
XLA Ops:
  7.2 1.2 slice.15
  9.0 1.3 collective-permute-start
  10.4 0.9 constant_dynamic-slice_fusion
  11.2 4.6 collective-permute-start.2
  15.8 1.0 slice.16
  16.8 1.3 collective-permute-start.1
  18.1 1.3 fusion.25
  20.1 0.7 iota_compare_fusion.6
  20.7 0.8 convert_reduce_fusion.1
  21.5 1.4 constant_dynamic-update-slice_fusion.1
  23.8 0.7 iota_compare_fusion
  24.7 1.4 fusion.14
  26.6 0.7 copy-done.4
  27.6 1.9 gather_fusion.3
  29.7 1.7 fusion.2
  31.3 76.0 %all-reduce.2.cloned.1.call-done = f32[140,1024]{1,0:T(8,128)} async-done(((f32[140,1024]{1,0:T(8,128)}), f32[140,1024]{1,0:T(8,128)}) %all-reduce.2.cloned.1.call-update) | async-done | bytes 573456 | tf_op jit(solution)/shard_map/psum | solution.py:112
  107.3 1.4 convolution_convert_fusion.3
  108.7 2.5 gather_fusion.6
  111.2 1.1 copy.47
  112.3 3.0 bitcast_reduce_fusion
  115.3 0.7 select_reduce_fusion
  116.0 2.3 gather_fusion.4
  118.2 1.1 copy.44
  119.7 2.3 gather_fusion.5
  122.0 1.1 copy.46
  123.2 1.7 fusion.5
  124.9 1.0 convert_multiply_fusion.2
  126.3 1.6 gather_fusion.7
  128.1 1.0 fusion.7
  129.5 1.2 convolution_divide_fusion
  130.7 2.3 fusion.32
  133.0 3.6 gather_fusion
  136.7 5.1 add_convert_fusion
  141.8 2.7 copy.50
  144.9 1.4 convolution_bitcast_fusion.3
  146.7 0.6 convolution_bitcast_fusion.2
  147.3 0.6 convolution_bitcast_fusion.1
  147.9 1.5 pad_maximum_fusion
  149.4 3.6 gather_fusion.2
  153.0 4.7 bitcast_select_fusion
  157.7 0.6 copy-done.12
  158.4 1.6 gather_fusion.1
  160.0 23.4 %reduce-scatter.7.cloned.1.call-done = bf16[128,768]{1,0:T(8,128)(2,1)} async-done(((bf16[1024,768]{1,0:T(8,128)(2,1)}), bf16[128,768]{1,0:T(8,128)(2,1)}) %reduce-scatter.7.cloned.1.call-update) | async-done | bytes 196624
  183.4 1.1 copy.51
  184.7 3.4 collective-permute-start.3
  188.7 1.0 collective-permute-done.3
  189.8 0.7 pad_maximum_fusion.1
  190.5 694.1 %reduce-scatter.5.cloned.1.call-done = f32[64,128]{1,0:T(8,128)} async-done(((f32[4096,128]{1,0:T(8,128)}), f32[64,128]{1,0:T(8,128)}) %reduce-scatter.5.cloned.1.call-update) | async-done | bytes 32784 | tf_op jit(solution)/shard_map/reduce_scatter | solution.py:157
  (73 shorter events, 4.9 us)
Async XLA Ops:
  7.2 17.5 %copy-start = (bf16[1024,512]{1,0:T(8,128)(2,1)S(1)}, bf16[1024,512]{1,0:T(8,128)(2,1)}, u32[]{:S(2)}) copy-start(bf16[1024,512]{1,0:T(8,128)(2,1)} %param.19) | copy-start | bytes 3145732
  7.2 17.4 %copy-start.7 = (bf16[80,512]{1,0:T(8,128)(2,1)S(1)}, bf16[80,512]{1,0:T(8,128)(2,1)}, u32[]{:S(2)}) copy-start(bf16[80,512]{1,0:T(8,128)(2,1)} %param.20) | copy-start | bytes 245764
  7.2 100.2 %all-reduce.2.cloned.1.call-start = ((), (), s32[]{:S(2)}) async-start(), calls=%async_computation.2 | async-start | bytes 1179648 | tf_op jit(solution)/shard_map/psum | solution.py:112
  9.0 14.6 %collective-permute-start = (bf16[128]{0:T(256)(128)(2,1)S(1)}, bf16[128]{0:T(256)(128)(2,1)S(1)}, u32[]{:S(2)}, u32[]{:S(2)}) collective-permute-start(bf16[128]{0:T(256)(128)(2,1)S(1)} %fusion.29), channel_id=1, source_target_pairs={{8,0},{16,8},{24,16},{32,24},{40,32},{48,40},{56,48},{64,56},{72,6... | collective-permute-start | bytes 776 | tf_op jit(solution)/shard_map/ppermute | solution.py:26
  11.2 13.4 %collective-permute-start.2 = (bf16[60,512]{1,0:T(8,128)(2,1)S(1)}, bf16[60,512]{1,0:T(8,128)(2,1)S(1)}, u32[]{:S(2)}, u32[]{:S(2)}) collective-permute-start(bf16[60,512]{1,0:T(8,128)(2,1)S(1)} %constant_dynamic-slice_fusion), channel_id=1, source_target_pairs={{0,8},{8,0},{16,24},{24,16},{32,40},{40,32},{48,56},{56,48},{64,72... | collective-permute-start | bytes 184328 | tf_op jit(solution)/shard_map/ppermute | solution.py:30
  16.8 9.4 %collective-permute-start.1 = (bf16[128,1024]{1,0:T(8,128)(2,1)S(1)}, bf16[128,1024]{1,0:T(8,128)(2,1)S(1)}, u32[]{:S(2)}, u32[]{:S(2)}) collective-permute-start(bf16[128,1024]{1,0:T(8,128)(2,1)S(1)} %slice.16), channel_id=1, source_target_pairs={{8,0},{16,8},{24,16},{32,24},{40,32},{48,40},{56,48},{64,56},{72,6... | collective-permute-start | bytes 786440 | tf_op jit(solution)/shard_map/ppermute | solution.py:26
  24.6 2.1 copy-start.11
  26.1 1.3 copy-start.8
  26.1 157.3 %reduce-scatter.7.cloned.1.call-start = ((), (), s32[]{:S(2)}) async-start(), calls=%async_computation.4 | async-start | bytes 1769472
  26.6 0.7 copy-start.4
  29.6 82.6 %copy-start.3 = (bf16[768,128]{0,1:T(8,128)(2,1)}, bf16[768,128]{0,1:T(8,128)(2,1)S(1)}, u32[]{:S(2)}) copy-start(bf16[768,128]{0,1:T(8,128)(2,1)S(1)} %copy.43) | copy-start | bytes 589828
  112.3 3.0 copy-start.6
  126.1 2.0 copy-start.10
  128.0 2.7 copy-start.5
  141.8 2.9 copy-start.13
  141.8 4.5 copy-start.1
  141.8 4.5 copy-start.9
  144.5 740.1 %reduce-scatter.5.cloned.1.call-start = ((), (), s32[]{:S(2)}) async-start(), calls=%async_computation.3 | async-start | bytes 2129920 | tf_op jit(solution)/shard_map/reduce_scatter | solution.py:157
  144.9 2.4 copy-start.2
  157.7 0.6 copy-start.12
  184.7 5.0 collective-permute-start.3
Sparse Core Ops, SparseCore 0:
  26.2 81.0 all-reduce.1
  144.6 38.7 reduce-scatter.6
  188.3 696.2 reduce-scatter.4
where the time goes:
time: 892 us; the launch traced here: 891 us
  waiting for transfers between devices  795 us (89%)
  local copies, waits for them, and re-layouts  32.8 us (4%)
  matrix products  21.3 us (2%)
  other arithmetic  15.9 us (2%)
  between operations  15.6 us (2%)
  starting transfers between devices  10.9 us (1%)
    reduce_scatter x1, waiting for transfers between devices, local(): lax.psum_scatter(ordered, 'seq', scatter_dimension=0, tiled=True)  694 us
    psum x1, waiting for transfers between devices, local(): lax.psum(jnp.dot(owner_rows, up_weight.T, preferred_element_type=fp), 'tp')  76 us
    unnamed x4, waiting for transfers between devices  23.4 us
  transfers between devices with their start and end apart: 7, of which 4 were waited for; matrix products, arithmetic and copies ran while one was open for 3% of the time, Pallas kernels for 0%

commit v1 on v0

v1 whole, which is shorter than its diff:
```python
import functools

import jax
import jax.numpy as jnp
from jax import lax
from jax.experimental import pallas as pl
from jax.experimental.pallas import tpu as pltpu
from jax.sharding import PartitionSpec as P

HEAD = 64
NY = 4
NEG = -1e30
F32 = jnp.float32
BF = jnp.bfloat16
NT = (((1,), (1,)), ((), ()))
TN = (((0,), (0,)), ((), ()))


def dot(a, b, dims=(((1,), (0,)), ((), ()))):
    return lax.dot_general(a, b, dims, preferred_element_type=F32)


def up16(n):
    return -(-n // 16) * 16


def row_of(mask, value):
    return jnp.sum(jnp.where(mask, value, 0.0), axis=0, keepdims=True)


def rows8(width, *rows):
    index = lax.broadcasted_iota(jnp.int32, (8, width), 0)
    out = jnp.zeros((8, width), F32)
    for i, row in enumerate(rows):
        out = jnp.where(index == i, row, out)
    return out


def z_order(nz):
    return sorted(range(1, nz), key=lambda d: -min(d, nz - d)) + [0]


def kernel(
    sizes,
    cols_ref, rows_ref, slots_ref, bytes_hbm, wq_hbm, wk_hbm, wv_hbm, wo_hbm, up_hbm, pg_hbm,
    byte_out, owned_out,
    bytes_ref, wq_ref, wk_ref, wv_ref, wo_ref, up_ref, pg_ref,
    bytes_t, k_ref, v_ref, pooled_ref, pooled_t, mt_ref, mix_ref, pb_ref, stack_ref,
    gm_send, gm_recv, mix_own, mix_prev, mix_next, mix_blk,
    a_send, a_recv, b_send, b_recv, d_send, d_recv,
    part_send, part_recv, part_own, y_send, y_recv, z_send, z_recv,
    load_sem, gm_ssem, gm_rsem, m_ssem, m_rsem, ag_ssem, ag_rsem,
    a_ssem, a_rsem, b_ssem, b_rsem, d_ssem, d_rsem,
    p_ssem, p_rsem, y_ssem, y_rsem, z_ssem, z_rsem,
):
    n_seq, ntp, pcap, rows_dev, window, chunks = sizes
    nz = n_seq // NY
    slots = mt_ref.shape[1]
    byte_dev, width = bytes_ref.shape
    cols = k_ref.shape[1]
    block = owned_out.shape[0]
    scale = HEAD ** -0.5
    s = lax.axis_index("seq")
    t = lax.axis_index("tp")
    y, z = lax.rem(s, NY), s // NY
    following, before = lax.rem(s + 1, n_seq), lax.rem(s + n_seq - 1, n_seq)
    order = z_order(nz)

    def tp_peer(o):
        return lax.rem(t + o, ntp)

    def y_peer(o):
        return z * NY + lax.rem(y + o, NY)

    def z_peer(o):
        return lax.rem(z + o, nz) * NY + y

    def send(src, dst, ssem, rsem, **where):
        return pltpu.make_async_remote_copy(
            src_ref=src, dst_ref=dst, send_sem=ssem, recv_sem=rsem,
            device_id=where, device_id_type=pl.DeviceIdType.MESH,
        )

    barrier = pltpu.get_barrier_semaphore()
    peers = [{"tp": tp_peer(o)} for o in range(1, ntp)]
    peers += [{"seq": following}, {"seq": before}]
    peers += [{"seq": y_peer(o)} for o in range(1, NY)]
    peers += [{"seq": z_peer(o)} for o in range(1, nz)]
    for peer in peers:
        pl.semaphore_signal(barrier, inc=1, device_id=peer, device_id_type=pl.DeviceIdType.MESH)

    loads = [
        pltpu.make_async_copy(src, dst, load_sem.at[i])
        for i, (src, dst) in enumerate([
            (pg_hbm, pg_ref), (up_hbm, up_ref), (bytes_hbm, bytes_ref), (wk_hbm, wk_ref),
            (wv_hbm, wv_ref), (wq_hbm, wq_ref), (wo_hbm, wo_ref),
        ])
    ]
    for load in loads:
        load.start()

    lo, hi = cols_ref[:, 0:1], cols_ref[:, 1:2]
    position = lax.broadcasted_iota(jnp.int32, (slots, byte_dev), 1)
    member = (position >= lo) & (position < hi)
    member_bf = jnp.where(member, 1.0, 0.0).astype(BF)
    position_t = lax.broadcasted_iota(jnp.int32, (byte_dev, slots), 0)
    member_t = (position_t >= rows_ref[0:1, :]) & (position_t < rows_ref[1:2, :])
    mt_ref[...] = jnp.where(member_t, 1.0, 0.0).astype(BF)
    slot = lax.broadcasted_iota(jnp.int32, (slots, 1), 0)
    used = (slot < pcap) & (lo < byte_dev)
    owned = jnp.sum(jnp.where(used, 1.0, 0.0), axis=0, keepdims=True).astype(jnp.int32)
    is_prev = slot == pcap
    is_last = slot == owned - 1
    count_own = (hi - lo).astype(F32)
    base = jnp.where(lax.rem(s, 2) == 0, 0, rows_dev - owned)
    wanted = base + jnp.where(is_prev, -1, slot)

    def select(first, size):
        row = lax.broadcasted_iota(jnp.int32, (slots, size), 1) + first
        return jnp.where((row == wanted) & (used | is_prev), 1.0, 0.0).astype(BF)

    loads[0].wait()
    loads[1].wait()
    pg = pg_ref[...]

    def mix_partial(j):
        return dot(pg, up_ref[pl.ds(pl.multiple_of(j * cols, cols), cols), :], NT)

    for o in range(1, ntp):
        gm_send[o - 1] = mix_partial(tp_peer(o)).astype(BF)
    pl.semaphore_wait(barrier, len(peers))
    gm_copies = [
        send(gm_send.at[o - 1], gm_recv.at[o - 1], gm_ssem.at[o - 1], gm_rsem.at[o - 1], tp=tp_peer(o))
        for o in range(1, ntp)
    ]
    for copy in gm_copies:
        copy.start()
    gm_own = mix_partial(t)

    def exchange(src, dst, ssem, rsem):
        copies = [
            send(src.at[0], dst.at[0], ssem.at[0], rsem.at[0], seq=following),
            send(src.at[1], dst.at[1], ssem.at[1], rsem.at[1], seq=before),
        ]
        for copy in copies:
            copy.start()
        return copies

    loads[2].wait()
    pooled_sum = dot(member_bf, bytes_ref[...])
    count_row = jnp.broadcast_to(row_of(is_last, count_own), (1, width))
    a_send[0] = rows8(width, row_of(is_last, pooled_sum), count_row)
    count_row = jnp.broadcast_to(row_of(is_prev, count_own), (1, width))
    a_send[1] = rows8(width, row_of(is_prev, pooled_sum), count_row)
    a_copies = exchange(a_send, a_recv, a_ssem, a_rsem)

    loads[3].wait()
    k_ref[...] = dot(bytes_ref[...], wk_ref[...]).astype(BF)
    loads[4].wait()
    v_ref[...] = dot(bytes_ref[...], wv_ref[...]).astype(BF)

    for copy in gm_copies:
        copy.wait()
    total = gm_own
    for o in range(1, ntp):
        total = total + gm_recv[o - 1].astype(F32)
    mix_own[...] = total.astype(BF)
    m_copies = [
        send(mix_own.at[pl.ds(rows_dev - window, window)], mix_prev, m_ssem.at[0], m_rsem.at[0], seq=following),
        send(mix_own.at[pl.ds(0, window)], mix_next, m_ssem.at[1], m_rsem.at[1], seq=before),
    ]
    for copy in m_copies:
        copy.start()

    for copy in a_copies:
        copy.wait()
    lane = lax.broadcasted_iota(jnp.int32, (1, cols), 1)
    head0 = lane < HEAD

    def merged(own, received, index):
        width_here = own.shape[1]
        extra = jnp.where(is_prev, received[0, index:index + 1, 0:width_here], 0.0)
        return own + extra + jnp.where(is_last, received[1, index:index + 1, 0:width_here], 0.0)

    pooled_sum = merged(pooled_sum, a_recv, 0)
    counts = jnp.maximum(merged(count_own, a_recv, 1), 1.0)
    pooled_ref[...] = (pooled_sum / counts).astype(BF)
    loads[5].wait()
    queries = dot(pooled_ref[...], wq_ref[...]).astype(BF)

    for copy in m_copies:
        copy.wait()
    picked = dot(select(0, rows_dev), mix_own[...])
    picked = picked + dot(select(-window, window), mix_prev[...])
    picked = picked + dot(select(rows_dev, window), mix_next[...])
    mix_blk[...] = picked.astype(BF)
    mine = pl.ds(pl.multiple_of(t * cols, cols), cols)
    ag_copies = [
        send(mix_blk, mix_ref.at[:, mine], ag_ssem.at[o - 1], ag_rsem.at[o - 1], tp=tp_peer(o))
        for o in range(1, ntp)
    ]
    for copy in ag_copies:
        copy.start()
    mix_ref[:, mine] = mix_blk[...]

    def heads(value):
        zero = jnp.zeros_like(value)
        return jnp.concatenate([jnp.where(head0, value, zero), jnp.where(head0, zero, value)], axis=0)

    def unheads(value):
        return jnp.where(head0, value[:slots], value[slots:])

    member2 = jnp.concatenate([member, member], axis=0)
    queries2 = heads(queries)
    scores = jnp.where(member2, dot(queries2, k_ref[...], NT) * scale, NEG)
    peak = jnp.max(scores, axis=1, keepdims=True)
    expo = jnp.where(member2, jnp.exp(scores - peak), 0.0)
    sums = unheads(jnp.sum(expo, axis=1, keepdims=True))
    peaks = unheads(peak)
    partial_out = unheads(dot(expo.astype(BF), v_ref[...]))
    for i, mask in enumerate((is_last, is_prev)):
        b_send[i] = rows8(cols, row_of(mask, partial_out), row_of(mask, peaks), row_of(mask, sums))
    b_copies = exchange(b_send, b_recv, b_ssem, b_rsem)
    bytes_t[...] = bytes_ref[...].T
    pooled_t[...] = pooled_ref[...].T
    for copy in b_copies:
        copy.wait()

    def received(index, empty):
        other = jnp.where(is_last, b_recv[1, index:index + 1, :], empty)
        return jnp.where(is_prev, b_recv[0, index:index + 1, :], other)

    other_peaks = received(1, NEG)
    top = jnp.maximum(peaks, other_peaks)
    keep, add = jnp.exp(peaks - top), jnp.exp(other_peaks - top)
    denom = sums * keep + received(2, 0.0) * add
    denom = jnp.where(denom > 0.0, denom, 1.0)
    attended = ((partial_out * keep + received(0, 0.0) * add) / denom).astype(BF)
    factor = keep / denom
    factor2 = jnp.concatenate([factor[:, 0:1], factor[:, HEAD:HEAD + 1]], axis=0)
    weights = expo * factor2

    def stack(i, value):
        count = width // block
        stack_ref[pl.ds(i * count, count)] = value.astype(BF).reshape(count, block, cols)

    loads[6].wait()
    for copy in ag_copies:
        copy.wait()
    grad_attended = dot(mix_ref[...], wo_ref[...], NT).astype(BF)
    grad2 = heads(grad_attended)
    delta = jnp.sum(grad2.astype(F32) * heads(attended).astype(F32), axis=1, keepdims=True)
    grad_scores = (weights * (dot(grad2, v_ref[...], NT) - delta)).astype(BF)
    grad_queries = unheads(dot(grad_scores, k_ref[...])) * scale
    for i, mask in enumerate((is_last, is_prev)):
        d_send[i] = rows8(cols, row_of(mask, grad_queries))
    d_copies = exchange(d_send, d_recv, d_ssem, d_rsem)
    grad_keys = (dot(grad_scores, queries2, TN) * scale).astype(BF)
    grad_values = dot(weights.astype(BF), grad2, TN).astype(BF)
    stack(1, dot(bytes_t[...], grad_keys))
    stack(2, dot(bytes_t[...], grad_values))
    counted = jnp.where(is_prev, jnp.zeros_like(attended), attended)
    stack(3, dot(mix_ref[...], counted, TN))
    for copy in d_copies:
        copy.wait()
    grad_queries = merged(grad_queries, d_recv, 0).astype(BF)
    counted = jnp.where(is_prev, jnp.zeros_like(grad_queries), grad_queries)
    stack(0, dot(pooled_t[...], counted))

    per = block * nz // chunks
    for i, o in enumerate(order):
        target = lax.rem(z + o, nz) * NY

        def reorder(q, _, i=i, target=target):
            y_send[q, pl.ds(i * block, block), :] = stack_ref[slots_ref[target + q]]
            return 0

        lax.fori_loop(0, NY, reorder, 0)
    y_copies = []
    for c in range(chunks):
        part = pl.ds(c * per, per)
        y_copies.append([
            send(
                y_send.at[lax.rem(y + o, NY), part], y_recv.at[o - 1, part],
                y_ssem.at[o - 1, c], y_rsem.at[o - 1, c], seq=y_peer(o),
            )
            for o in range(1, NY)
        ])
        for copy in y_copies[-1]:
            copy.start()

    pb_ref[...] = (dot(grad_queries, wq_ref[...], NT) / counts).astype(BF)

    def byte_partial(j):
        columns = pl.ds(pl.multiple_of(j * cols, cols), cols)
        value = dot(grad_keys, wk_ref[columns, :], NT) + dot(grad_values, wv_ref[columns, :], NT)
        return value + dot(mt_ref[...], pb_ref[:, columns])

    p_copies = []
    for o in range(1, ntp):
        part_send[o - 1] = byte_partial(tp_peer(o)).astype(BF)
        p_copies.append(send(
            part_send.at[o - 1], part_recv.at[o - 1], p_ssem.at[o - 1], p_rsem.at[o - 1], tp=tp_peer(o),
        ))
        p_copies[-1].start()
    mix_mean = (mix_blk[...].astype(F32) / counts).astype(BF)
    part_own[...] = byte_partial(t) + dot(mt_ref[...], mix_mean)

    z_copies = []
    for c in range(chunks):
        for copy in y_copies[c]:
            copy.wait()
        part = pl.ds(c * per, per)
        summed = y_send[y, part, :].astype(F32)
        for o in range(1, NY):
            summed = summed + y_recv[o - 1, part, :].astype(F32)
        z_send[part, :] = summed.astype(BF)
        for i in range(c * nz // chunks, (c + 1) * nz // chunks):
            if order[i]:
                z_copies.append(send(
                    z_send.at[pl.ds(i * block, block)], z_recv.at[i], z_ssem.at[i], z_rsem.at[i],
                    seq=z_peer(order[i]),
                ))
                z_copies[-1].start()

    total = part_own[...]
    for o in range(1, ntp):
        p_copies[o - 1].wait()
        total = total + part_recv[o - 1].astype(F32)
    byte_out[...] = total.astype(BF)

    total = z_send[pl.ds((nz - 1) * block, block), :].astype(F32)
    for i, copy in enumerate(z_copies):
        copy.wait()
        total = total + z_recv[i].astype(F32)
    owned_out[...] = total


def local(
    byte_states, patch_starts, query_weight, key_weight, value_weight, out_weight, up_weight, patch_grad,
    owner_slots, *, n_seq, ntp,
):
    byte_dev, width = byte_states.shape
    pcap = patch_starts.shape[0]
    rows_dev, features = patch_grad.shape
    cols = query_weight.shape[1]
    slots = up16(pcap + 1)
    window = up16(pcap - rows_dev + 1)
    nz = n_seq // NY
    chunks = 4 if nz % 4 == 0 else nz
    block = 4 * width // n_seq
    fill = jnp.full((slots - pcap - 1,), byte_dev, jnp.int32)
    lo = jnp.concatenate([patch_starts, jnp.zeros((1,), jnp.int32), fill])
    hi = jnp.concatenate([patch_starts[1:], jnp.full((1,), byte_dev, jnp.int32), patch_starts[:1], fill])
    edges = jnp.stack([lo, hi])
    vmem = pl.BlockSpec(memory_space=pltpu.VMEM)
    hbm = pl.BlockSpec(memory_space=pl.ANY)
    dma = pltpu.SemaphoreType.DMA
    pairs = [dma((2,))] * 2
    return pl.pallas_call(
        functools.partial(kernel, (n_seq, ntp, pcap, rows_dev, window, chunks)),
        out_shape=(
            jax.ShapeDtypeStruct((byte_dev, cols), BF),
            jax.ShapeDtypeStruct((block, cols), F32),
        ),
        in_specs=[vmem, vmem, pl.BlockSpec(memory_space=pltpu.SMEM)] + [hbm] * 7,
        out_specs=(vmem, vmem),
        scratch_shapes=[
            pltpu.VMEM((byte_dev, width), BF),
            pltpu.VMEM((width, cols), BF),
            pltpu.VMEM((width, cols), BF),
            pltpu.VMEM((width, cols), BF),
            pltpu.VMEM((cols, width), BF),
            pltpu.VMEM((width, features), BF),
            pltpu.VMEM((rows_dev, features), BF),
            pltpu.VMEM((width, byte_dev), BF),
            pltpu.VMEM((byte_dev, cols), BF),
            pltpu.VMEM((byte_dev, cols), BF),
            pltpu.VMEM((slots, width), BF),
            pltpu.VMEM((width, slots), BF),
            pltpu.VMEM((byte_dev, slots), BF),
            pltpu.VMEM((slots, width), BF),
            pltpu.VMEM((slots, width), BF),
            pltpu.VMEM((n_seq, block, cols), BF),
            pltpu.VMEM((ntp - 1, rows_dev, cols), BF),
            pltpu.VMEM((ntp - 1, rows_dev, cols), BF),
            pltpu.VMEM((rows_dev, cols), BF),
            pltpu.VMEM((window, cols), BF),
            pltpu.VMEM((window, cols), BF),
            pltpu.VMEM((slots, cols), BF),
            pltpu.VMEM((2, 8, width), F32),
            pltpu.VMEM((2, 8, width), F32),
            pltpu.VMEM((2, 8, cols), F32),
            pltpu.VMEM((2, 8, cols), F32),
            pltpu.VMEM((2, 8, cols), F32),
            pltpu.VMEM((2, 8, cols), F32),
            pltpu.VMEM((ntp - 1, byte_dev, cols), BF),
            pltpu.VMEM((ntp - 1, byte_dev, cols), BF),
            pltpu.VMEM((byte_dev, cols), F32),
            pltpu.VMEM((NY, nz * block, cols), BF),
            pltpu.VMEM((NY - 1, nz * block, cols), BF),
            pltpu.VMEM((nz * block, cols), BF),
            pltpu.VMEM((nz - 1, block, cols), BF),
            dma((7,)),
            dma((ntp - 1,)), dma((ntp - 1,)),
            *pairs,
            dma((ntp - 1,)), dma((ntp - 1,)),
            *pairs, *pairs, *pairs,
            dma((ntp - 1,)), dma((ntp - 1,)),
            dma((NY - 1, chunks)), dma((NY - 1, chunks)),
            dma((nz - 1,)), dma((nz - 1,)),
        ],
        compiler_params=pltpu.CompilerParams(
            collective_id=0, has_side_effects=True, vmem_limit_bytes=48 * 1024 * 1024
        ),
    )(
        edges.T, jnp.pad(edges, ((0, 6), (0, 0))), owner_slots, byte_states, query_weight, key_weight,
        value_weight, out_weight, up_weight, patch_grad,
    )


def solution(mesh):
    in_specs = (
        P("seq", None),
        P("seq"),
        P(None, "tp"),
        P(None, "tp"),
        P(None, "tp"),
        P("tp", None),
        P(None, "tp"),
        P("seq", "tp"),
        P(),
    )
    out_specs = (P("seq", "tp"), P("seq", "tp"))
    step = functools.partial(local, n_seq=mesh.shape["seq"], ntp=mesh.shape["tp"])
    return jax.shard_map(step, mesh=mesh, in_specs=in_specs, out_specs=out_specs, check_vma=False)
```

time: 892 us -> 68.7 us (0.08)
  the two profiles are of different devices: /device:TPU:6 before, /device:TPU:1 now
where the time goes in v1:
time: 68.7 us; the launch traced here: 68.3 us
  Pallas kernels  55 us (80%)
  local copies, waits for them, and re-layouts  11.2 us (16%)
  other arithmetic  1.41 us (2%)
    pallas_call x1, Pallas kernels, local(): pl.pallas_call(functools.partial(kernel, (n_seq, ntp, pcap, rows_dev, win...  55 us
    unnamed x18, local copies, waits for them, and re-layouts  9.16 us
    concatenate x1, other arithmetic, local(): lo = jnp.concatenate([patch_starts, jnp.zeros((1,), jnp.int32), fill])  1.4 us

profile of v1, /device:TPU:1, one launch (start us, length us, event | category | flops | bytes accessed | tf_op | source)
XLA Modules:
  0.0 68.3 jit_solution(3848077891669405923)
XLA Ops:
  0.6 1.2 %slice.7 = s32[1]{0:T(128)} slice(s32[140]{0:T(256)} %param.10), slice={[0:1]} | slice | bytes 8 | tf_op jit(solution)/shard_map/slice | solution.py:354
  1.8 0.7 %slice.6 = s32[139]{0:T(256)S(1)} slice(s32[140]{0:T(256)} %param.10), slice={[1:140]} | slice | bytes 1112 | tf_op jit(solution)/shard_map/slice | solution.py:354
  2.6 1.4 %pad_add_fusion.2 = (s32[144]{0:T(256)S(1)}, s32[144]{0:T(256)S(1)}) fusion(s32[3]{0:T(128)S(1)} %broadcast.5, s32[1]{0:T(128)} %constant.0.clone.1, s32[140]{0:T(256)} %param.10, s32[1]{0:T(128)} %slice.7, s32[1]{0:T(128)} %constant.2.clone.1, s32[139]{0:T(256)S(1)} %slice.6), kind=kLoop, calls=%fused_computation.2 | loop fusion | flops 720 | bytes 2292 | tf_op jit(solution)/shard_map/concatenate | solution.py:353
  4.0 0.1 copy.11.cols_ref
  4.1 0.0 copy-start
  4.1 1.3 %copy-done = bf16[640,1024]{1,0:T(8,128)(2,1)S(1)} copy-done((bf16[640,1024]{1,0:T(8,128)(2,1)S(1)}, bf16[640,1024]{1,0:T(8,128)(2,1)}, u32[]{:S(2)}) %copy-start) | copy-done | bytes 1310744
  5.4 0.0 copy-start.1
  5.4 1.2 %copy-done.1 = bf16[1024,512]{1,0:T(8,128)(2,1)S(1)} copy-done((bf16[1024,512]{1,0:T(8,128)(2,1)S(1)}, bf16[1024,512]{1,0:T(8,128)(2,1)}, u32[]{:S(2)}) %copy-start.1) | copy-done | bytes 1048600
  6.7 0.0 copy-start.2
  6.7 0.9 %copy-done.2 = bf16[1024,128]{1,0:T(8,128)(2,1)S(1)} copy-done((bf16[1024,128]{1,0:T(8,128)(2,1)S(1)}, bf16[1024,128]{1,0:T(8,128)(2,1)}, u32[]{:S(2)}) %copy-start.2) | copy-done | bytes 262168
  7.6 0.0 copy-start.3
  7.6 0.9 %copy-done.3 = bf16[1024,128]{1,0:T(8,128)(2,1)S(1)} copy-done((bf16[1024,128]{1,0:T(8,128)(2,1)S(1)}, bf16[1024,128]{1,0:T(8,128)(2,1)}, u32[]{:S(2)}) %copy-start.3) | copy-done | bytes 262168
  8.6 0.0 copy-start.4
  8.6 0.9 %copy-done.4 = bf16[1024,128]{1,0:T(8,128)(2,1)S(1)} copy-done((bf16[1024,128]{1,0:T(8,128)(2,1)S(1)}, bf16[1024,128]{1,0:T(8,128)(2,1)}, u32[]{:S(2)}) %copy-start.4) | copy-done | bytes 262168
  9.5 0.0 copy-start.5
  9.5 0.9 %copy-done.5 = bf16[128,1024]{1,0:T(8,128)(2,1)S(1)} copy-done((bf16[128,1024]{1,0:T(8,128)(2,1)S(1)}, bf16[128,1024]{1,0:T(8,128)(2,1)}, u32[]{:S(2)}) %copy-start.5) | copy-done | bytes 262168
  10.5 0.0 copy-start.6
  10.5 0.9 %copy-done.6 = bf16[80,512]{1,0:T(8,128)(2,1)S(1)} copy-done((bf16[80,512]{1,0:T(8,128)(2,1)S(1)}, bf16[80,512]{1,0:T(8,128)(2,1)}, u32[]{:S(2)}) %copy-start.6) | copy-done | bytes 81944
  11.3 0.0 copy-start.7
  11.3 0.7 copy-done.7
  12.0 55.0 %shard_map.104 = (bf16[640,128]{1,0:T(8,128)(2,1)S(1)}, f32[64,128]{1,0:T(8,128)S(1)}) custom-call(s32[144,2]{1,0:T(8,128)S(1)} %copy.11.cols_ref, s32[8,144]{1,0:T(8,128)S(1)} %pad.4.rows_ref, s32[64]{0:T(128)S(1)} %copy-done.7, bf16[640,1024]{1,0:T(8,128)(2,1)S(1)} %copy-done, bf16[1024,128]{1,0:T(8,128)(2,1)S(1)} %copy-done.2, ...), custom_call_target="tpu_custom_call" | custom-call | tf_op jit(solution)/shard_map/pallas_call | solution.py:360
  67.0 0.7 copy.14
  67.6 0.6 copy.15
  (3 shorter events, 0.0 us)
Async XLA Ops:
  4.1 1.3 %copy-start = (bf16[640,1024]{1,0:T(8,128)(2,1)S(1)}, bf16[640,1024]{1,0:T(8,128)(2,1)}, u32[]{:S(2)}) copy-start(bf16[640,1024]{1,0:T(8,128)(2,1)} %bytes_hbm.1) | copy-start | bytes 3932164
  5.4 1.2 %copy-start.1 = (bf16[1024,512]{1,0:T(8,128)(2,1)S(1)}, bf16[1024,512]{1,0:T(8,128)(2,1)}, u32[]{:S(2)}) copy-start(bf16[1024,512]{1,0:T(8,128)(2,1)} %up_hbm.1) | copy-start | bytes 3145732
  6.7 0.9 %copy-start.2 = (bf16[1024,128]{1,0:T(8,128)(2,1)S(1)}, bf16[1024,128]{1,0:T(8,128)(2,1)}, u32[]{:S(2)}) copy-start(bf16[1024,128]{1,0:T(8,128)(2,1)} %wq_hbm.1) | copy-start | bytes 786436
  7.6 0.9 %copy-start.3 = (bf16[1024,128]{1,0:T(8,128)(2,1)S(1)}, bf16[1024,128]{1,0:T(8,128)(2,1)}, u32[]{:S(2)}) copy-start(bf16[1024,128]{1,0:T(8,128)(2,1)} %wk_hbm.1) | copy-start | bytes 786436
  8.6 0.9 %copy-start.4 = (bf16[1024,128]{1,0:T(8,128)(2,1)S(1)}, bf16[1024,128]{1,0:T(8,128)(2,1)}, u32[]{:S(2)}) copy-start(bf16[1024,128]{1,0:T(8,128)(2,1)} %wv_hbm.1) | copy-start | bytes 786436
  9.5 0.9 %copy-start.5 = (bf16[128,1024]{1,0:T(8,128)(2,1)S(1)}, bf16[128,1024]{1,0:T(8,128)(2,1)}, u32[]{:S(2)}) copy-start(bf16[128,1024]{1,0:T(8,128)(2,1)} %wo_hbm.1) | copy-start | bytes 786436
  10.5 0.9 %copy-start.6 = (bf16[80,512]{1,0:T(8,128)(2,1)S(1)}, bf16[80,512]{1,0:T(8,128)(2,1)}, u32[]{:S(2)}) copy-start(bf16[80,512]{1,0:T(8,128)(2,1)} %pg_hbm.1) | copy-start | bytes 245764
  11.3 0.7 copy-start.7

commit v2 on v1

--- a/solution.py
+++ b/solution.py
@@ -42,7 +42,7 @@
 
 def kernel(
     sizes,
-    cols_ref, rows_ref, slots_ref, bytes_hbm, wq_hbm, wk_hbm, wv_hbm, wo_hbm, up_hbm, pg_hbm,
+    starts_ref, slots_ref, bytes_hbm, wq_hbm, wk_hbm, wv_hbm, wo_hbm, up_hbm, pg_hbm,
     byte_out, owned_out,
     bytes_ref, wq_ref, wk_ref, wv_ref, wo_ref, up_ref, pg_ref,
     bytes_t, k_ref, v_ref, pooled_ref, pooled_t, mt_ref, mix_ref, pb_ref, stack_ref,
@@ -99,14 +99,18 @@
     for load in loads:
         load.start()
 
-    lo, hi = cols_ref[:, 0:1], cols_ref[:, 1:2]
+    starts = starts_ref[...].astype(F32)
+    slot = lax.broadcasted_iota(jnp.int32, (slots, 1), 0)
+    nth = lax.broadcasted_iota(jnp.int32, (slots, pcap), 1)
+    lo = jnp.sum(jnp.where(nth == slot, starts, 0.0), axis=1, keepdims=True).astype(jnp.int32)
+    lo = jnp.where(slot > pcap, byte_dev, lo)
+    after = jnp.where(slot == pcap, 0, slot + 1)
+    hi = jnp.sum(jnp.where(nth == after, starts, 0.0), axis=1, keepdims=True).astype(jnp.int32)
+    hi = jnp.where((slot > pcap) | (slot == pcap - 1), byte_dev, hi)
     position = lax.broadcasted_iota(jnp.int32, (slots, byte_dev), 1)
     member = (position >= lo) & (position < hi)
     member_bf = jnp.where(member, 1.0, 0.0).astype(BF)
-    position_t = lax.broadcasted_iota(jnp.int32, (byte_dev, slots), 0)
-    member_t = (position_t >= rows_ref[0:1, :]) & (position_t < rows_ref[1:2, :])
-    mt_ref[...] = jnp.where(member_t, 1.0, 0.0).astype(BF)
-    slot = lax.broadcasted_iota(jnp.int32, (slots, 1), 0)
+    mt_ref[...] = member_bf.T
     used = (slot < pcap) & (lo < byte_dev)
     owned = jnp.sum(jnp.where(used, 1.0, 0.0), axis=0, keepdims=True).astype(jnp.int32)
     is_prev = slot == pcap
@@ -349,12 +353,8 @@
     nz = n_seq // NY
     chunks = 4 if nz % 4 == 0 else nz
     block = 4 * width // n_seq
-    fill = jnp.full((slots - pcap - 1,), byte_dev, jnp.int32)
-    lo = jnp.concatenate([patch_starts, jnp.zeros((1,), jnp.int32), fill])
-    hi = jnp.concatenate([patch_starts[1:], jnp.full((1,), byte_dev, jnp.int32), patch_starts[:1], fill])
-    edges = jnp.stack([lo, hi])
     vmem = pl.BlockSpec(memory_space=pltpu.VMEM)
-    hbm = pl.BlockSpec(memory_space=pl.ANY)
+    hbm = pl.BlockSpec(memory_space=pltpu.HBM)
     dma = pltpu.SemaphoreType.DMA
     pairs = [dma((2,))] * 2
     return pl.pallas_call(
@@ -363,7 +363,7 @@
             jax.ShapeDtypeStruct((byte_dev, cols), BF),
             jax.ShapeDtypeStruct((block, cols), F32),
         ),
-        in_specs=[vmem, vmem, pl.BlockSpec(memory_space=pltpu.SMEM)] + [hbm] * 7,
+        in_specs=[vmem, pl.BlockSpec(memory_space=pltpu.SMEM)] + [hbm] * 7,
         out_specs=(vmem, vmem),
         scratch_shapes=[
             pltpu.VMEM((byte_dev, width), BF),
@@ -411,11 +411,11 @@
             dma((nz - 1,)), dma((nz - 1,)),
         ],
         compiler_params=pltpu.CompilerParams(
-            collective_id=0, has_side_effects=True, vmem_limit_bytes=48 * 1024 * 1024
+            collective_id=0, has_side_effects=True, vmem_limit_bytes=62 * 1024 * 1024
         ),
     )(
-        edges.T, jnp.pad(edges, ((0, 6), (0, 0))), owner_slots, byte_states, query_weight, key_weight,
-        value_weight, out_weight, up_weight, patch_grad,
+        patch_starts.reshape(1, pcap), owner_slots, byte_states, query_weight, key_weight, value_weight,
+        out_weight, up_weight, patch_grad,
     )
 
 

time: 68.7 us -> 59.7 us (0.87)
  local copies, waits for them, and re-layouts: 11.2 us -> 2.97 us
  other arithmetic: 1.41 us -> 0 us
  Pallas kernels: 55 us -> 55.8 us
    unnamed x18 -> x2, local copies, waits for them, and re-layouts: 9.16 us -> 2.97 us
    slice x2 -> x0, local copies, waits for them, and re-layouts: 1.94 us -> none  [the longest x1 1.19 us: local(): patch_starts[:1]]
    concatenate x1 -> x0, other arithmetic: 1.4 us -> none  [local(): lo = jnp.concatenate([patch_starts, jnp.zeros((1,), jnp.int32), fill])]
    pallas_call x1, Pallas kernels: 55 us -> 55.8 us  [local(): pl.pallas_call(functools.partial(kernel, (n_seq, ntp, pcap, rows_dev, win...]
where the time goes in v2:
time: 59.7 us; the launch traced here: 59.4 us
  Pallas kernels  55.8 us (93%)
  local copies, waits for them, and re-layouts  2.97 us (5%)
  between operations  0.64 us (1%)
    pallas_call x1, Pallas kernels, local(): pl.pallas_call(functools.partial(kernel, (n_seq, ntp, pcap, rows_dev, win...  55.8 us
    unnamed x2, local copies, waits for them, and re-layouts  2.97 us

profile of v2, /device:TPU:1, one launch (start us, length us, event | category | flops | bytes accessed | tf_op | source)
XLA Modules:
  0.0 59.4 jit_solution(17355088440909342108)
XLA Ops:
  0.6 55.8 %shard_map.104 = (bf16[640,128]{1,0:T(8,128)(2,1)}, f32[64,128]{1,0:T(8,128)}) custom-call(s32[1,140]{1,0:T(1,128)} %bitcast.1, s32[64]{0:T(128)} %slots_ref.1, bf16[640,1024]{1,0:T(8,128)(2,1)} %bytes_hbm.1, bf16[1024,128]{1,0:T(8,128)(2,1)} %wq_hbm.1, bf16[1024,128]{1,0:T(8,128)(2,1)} %wk_hbm.1, bf16[1024,128]{1,0:T(8,128)(2,1)} %wv_hbm.1, ...), custom_call_target="tpu_custom_call" | custom-call | tf_op jit(solution)/shard_map/pallas_call | solution.py:360
  56.5 1.6 %copy.13 = bf16[640,128]{1,0:T(8,128)(2,1)} copy(bf16[640,128]{1,0:T(8,128)(2,1)} %get-tuple-element.4) | data formatting | bytes 327680
  58.1 1.4 %copy.14 = f32[64,128]{1,0:T(8,128)} copy(f32[64,128]{1,0:T(8,128)} %get-tuple-element.5) | data formatting | bytes 65536

commit v3 on v2

v3 whole, which is shorter than its diff:
```python
import functools

import jax
import jax.numpy as jnp
from jax import lax
from jax.experimental import pallas as pl
from jax.experimental.pallas import tpu as pltpu
from jax.sharding import PartitionSpec as P

HEAD = 64
NY = 4
NEG = -1e30
F32 = jnp.float32
BF = jnp.bfloat16
NT = (((1,), (1,)), ((), ()))
TN = (((0,), (0,)), ((), ()))


def dot(a, b, dims=(((1,), (0,)), ((), ()))):
    return lax.dot_general(a, b, dims, preferred_element_type=F32)


def up16(n):
    return -(-n // 16) * 16


def row_of(mask, value):
    return jnp.sum(jnp.where(mask, value, 0.0), axis=0, keepdims=True)


def rows8(width, *rows):
    index = lax.broadcasted_iota(jnp.int32, (8, width), 0)
    out = jnp.zeros((8, width), F32)
    for i, row in enumerate(rows):
        out = jnp.where(index == i, row, out)
    return out


def z_chunks(nz):
    if nz == 16:
        return [[8, 7, -7], [6, -6, 5, -5], [4, -4, 3, -3], [2, -2, 1, -1, 0]]
    return [[2], [1, -1], [0]]


def x_order(nx):
    return sorted(range(1, nx), key=lambda d: -min(d, nx - d)) + [0]


def kernel(
    sizes,
    starts_ref, slots_ref, bytes_hbm, wq_hbm, wk_hbm, wv_hbm, wo_hbm, up_hbm, pg_hbm,
    byte_out, owned_out,
    bytes_ref, wq_ref, wk_ref, wv_ref, wo_ref, up_ref, pg_ref,
    bytes_t, k_ref, v_ref, gk_ref, gv_ref, pooled_ref, pooled_t, mt_ref, mix_ref, pb_ref, stack_ref,
    gm_first, gm_send, gm_recv, mix_own, mix_buf,
    a_send, a_recv, b_send, b_recv,
    part, mate_recv, px_send, px_recv, y_send, y_far, y_dir, z_send, zf_recv, z_recv,
    load_sem, gm_ssem, gm_rsem, ag_ssem, ag_rsem, a_ssem, a_rsem, b_ssem, b_rsem,
    p_ssem, p_rsem, px_ssem, px_rsem, y_ssem, y_rsem, zf_ssem, zf_rsem, z_ssem, z_rsem,
):
    n_seq, ntp, pcap, rows_dev, window = sizes
    nz, nx = n_seq // NY, ntp // 2
    reach = nz // 4
    slots = mt_ref.shape[1]
    byte_dev, width = bytes_ref.shape
    cols = k_ref.shape[1]
    block = owned_out.shape[0]
    scale = HEAD ** -0.5
    s = lax.axis_index("seq")
    t = lax.axis_index("tp")
    y, z = lax.rem(s, NY), s // NY
    x, core = t // 2, lax.rem(t, 2)
    odd = lax.rem(s, 2)
    following, before = lax.rem(s + 1, n_seq), lax.rem(s + n_seq - 1, n_seq)
    partner = s + 1 - 2 * odd
    plus, minus = z * NY + lax.rem(y + 1, NY), z * NY + lax.rem(y + NY - 1, NY)
    chunks = z_chunks(nz)
    order = [o for chunk in chunks for o in chunk]
    near = [o for o in order if 0 < abs(o) <= reach]
    far = [o for o in order if abs(o) > reach]
    mine = pl.ds(pl.multiple_of(t * cols, cols), cols)
    my_half = pl.ds(pl.multiple_of(core * cols, cols), cols)
    mate_half = pl.ds(pl.multiple_of((1 - core) * cols, cols), cols)
    everyone = [(o, d) for o in x_order(nx) for d in (0, 1)]
    others = [pair for pair in everyone if pair != (0, 0)]

    def tp_peer(o, d):
        return 2 * lax.rem(x + o, nx) + lax.rem(core + d, 2)

    def z_peer(o):
        return lax.rem(z + o + nz, nz) * NY + y

    def send(src, dst, ssem, rsem, **where):
        return pltpu.make_async_remote_copy(
            src_ref=src, dst_ref=dst, send_sem=ssem, recv_sem=rsem,
            device_id=where, device_id_type=pl.DeviceIdType.MESH,
        )

    loads = [
        pltpu.make_async_copy(src, dst, load_sem.at[i])
        for i, (src, dst) in enumerate([
            (pg_hbm, pg_ref), (up_hbm, up_ref), (bytes_hbm, bytes_ref), (wk_hbm, wk_ref),
            (wv_hbm, wv_ref), (wq_hbm, wq_ref), (wo_hbm, wo_ref),
        ])
    ]
    for load in loads:
        load.start()

    barrier = pltpu.get_barrier_semaphore()
    peers = [{"tp": tp_peer(o, d)} for o, d in others]
    peers += [{"seq": partner, "tp": tp_peer(o, d)} for o, d in everyone]
    peers += [{"seq": before, "tp": tp_peer(o, d)} for o, d in everyone]
    peers += [{"seq": following}, {"seq": plus}, {"seq": minus}]
    peers += [{"seq": z_peer(o)} for o in near]
    for peer in peers:
        pl.semaphore_signal(barrier, inc=1, device_id=peer, device_id_type=pl.DeviceIdType.MESH)

    loads[0].wait()
    loads[1].wait()
    for o in x_order(nx):
        rows = pl.ds(pl.multiple_of(lax.rem(x + o, nx) * 2 * cols, 2 * cols), 2 * cols)
        value = dot(pg_ref[...], up_ref[rows, :], NT)
        if o == 0:
            gm_first[...] = value
        gm_send[o] = value.astype(BF)
    pl.semaphore_wait(barrier, len(peers))
    gm_copies = []
    for k, (o, d) in enumerate(others):
        half = mate_half if d else my_half
        gm_copies.append(send(gm_send.at[o, :, half], gm_recv.at[k], gm_ssem.at[k], gm_rsem.at[k], tp=tp_peer(o, d)))
        gm_copies[-1].start()

    starts = starts_ref[...].astype(F32)
    slot = lax.broadcasted_iota(jnp.int32, (slots, 1), 0)
    nth = lax.broadcasted_iota(jnp.int32, (slots, pcap), 1)
    lo = jnp.sum(jnp.where(nth == slot, starts, 0.0), axis=1, keepdims=True).astype(jnp.int32)
    lo = jnp.where(slot > pcap, byte_dev, lo)
    after = jnp.where(slot == pcap, 0, slot + 1)
    hi = jnp.sum(jnp.where(nth == after, starts, 0.0), axis=1, keepdims=True).astype(jnp.int32)
    hi = jnp.where((slot > pcap) | (slot == pcap - 1), byte_dev, hi)
    position = lax.broadcasted_iota(jnp.int32, (slots, byte_dev), 1)
    member = (position >= lo) & (position < hi)
    member_bf = jnp.where(member, 1.0, 0.0).astype(BF)
    mt_ref[...] = member_bf.T
    used = (slot < pcap) & (lo < byte_dev)
    owned = jnp.sum(jnp.where(used, 1.0, 0.0), axis=0, keepdims=True).astype(jnp.int32)
    is_prev = slot == pcap
    is_last = slot == owned - 1
    count_own = (hi - lo).astype(F32)

    def exchange(src, dst, ssem, rsem):
        copies = [
            send(src.at[0], dst.at[0], ssem.at[0], rsem.at[0], seq=following),
            send(src.at[1], dst.at[1], ssem.at[1], rsem.at[1], seq=before),
        ]
        for copy in copies:
            copy.start()
        return copies

    loads[2].wait()
    pooled_sum = dot(member_bf, bytes_ref[...])
    for i, mask in enumerate((is_last, is_prev)):
        count_row = jnp.broadcast_to(row_of(mask, count_own), (1, width))
        a_send[i] = rows8(width, row_of(mask, pooled_sum), count_row)
    a_copies = exchange(a_send, a_recv, a_ssem, a_rsem)

    loads[3].wait()
    k_ref[...] = dot(bytes_ref[...], wk_ref[...]).astype(BF)
    loads[4].wait()
    v_ref[...] = dot(bytes_ref[...], wv_ref[...]).astype(BF)

    for copy in gm_copies:
        copy.wait()
    total = gm_first[:, my_half]
    for k in range(len(others)):
        total = total + gm_recv[k].astype(F32)
    mix_own[...] = total.astype(BF)
    shared = pl.ds(pl.multiple_of((rows_dev - window) * (1 - odd), 16), window)
    ag_copies = []
    for k, (o, d) in enumerate(everyone):
        routes = [
            (mix_own.at[shared], pl.ds(rows_dev, window), partner),
            (mix_own.at[pl.ds(rows_dev - 16, 16)], pl.ds(rows_dev + window, 16), following),
        ]
        if (o, d) != (0, 0):
            routes.append((mix_own, pl.ds(0, rows_dev), s))
        for i, (src, rows, seq) in enumerate(routes):
            ag_copies.append(send(
                src, mix_buf.at[rows, mine], ag_ssem.at[i, k], ag_rsem.at[i, k], seq=seq, tp=tp_peer(o, d),
            ))
            ag_copies[-1].start()
    mix_buf[pl.ds(0, rows_dev), mine] = mix_own[...]

    for copy in a_copies:
        copy.wait()
    lane = lax.broadcasted_iota(jnp.int32, (1, cols), 1)
    head0 = lane < HEAD

    def merged(own, received, index):
        width_here = own.shape[1]
        extra = jnp.where(is_prev, received[0, index:index + 1, 0:width_here], 0.0)
        return own + extra + jnp.where(is_last, received[1, index:index + 1, 0:width_here], 0.0)

    pooled_sum = merged(pooled_sum, a_recv, 0)
    counts = jnp.maximum(merged(count_own, a_recv, 1), 1.0)
    pooled_ref[...] = (pooled_sum / counts).astype(BF)
    loads[5].wait()
    queries = dot(pooled_ref[...], wq_ref[...]).astype(BF)

    def heads(value):
        zero = jnp.zeros_like(value)
        return jnp.concatenate([jnp.where(head0, value, zero), jnp.where(head0, zero, value)], axis=0)

    def unheads(value):
        half = value.shape[0] // 2
        return jnp.where(head0, value[:half], value[half:])

    member2 = jnp.concatenate([member, member], axis=0)
    queries2 = heads(queries)
    scores = jnp.where(member2, dot(queries2, k_ref[...], NT) * scale, NEG)
    peak = jnp.max(scores, axis=1, keepdims=True)
    expo = jnp.where(member2, jnp.exp(scores - peak), 0.0)
    expo_bf = expo.astype(BF)
    sums = unheads(jnp.sum(expo, axis=1, keepdims=True))
    peaks = unheads(peak)
    partial_out = unheads(dot(expo_bf, v_ref[...]))
    partial_keys = unheads(dot(expo_bf, k_ref[...]))
    chosen = [
        heads(jnp.broadcast_to(jnp.where(mask, 1.0, 0.0), (slots, cols)).astype(BF)) for mask in (is_last, is_prev)
    ]
    spread = dot(expo_bf, jnp.concatenate(chosen, axis=1), TN)
    values = v_ref[...].astype(F32)
    spread = (spread * jnp.concatenate([values, values], axis=1)).astype(BF)
    products = dot(spread, k_ref[...], TN)
    for i, mask in enumerate((is_last, is_prev)):
        b_send[i, 0:8, :] = rows8(
            cols, row_of(mask, partial_out), row_of(mask, peaks), row_of(mask, sums), row_of(mask, partial_keys),
        )
        b_send[i, 8:8 + HEAD, :] = unheads(products[i * cols:(i + 1) * cols])
    b_copies = exchange(b_send, b_recv, b_ssem, b_rsem)
    bytes_t[...] = bytes_ref[...].T
    pooled_t[...] = pooled_ref[...].T
    for copy in b_copies:
        copy.wait()

    def received(index, empty):
        other = jnp.where(is_last, b_recv[1, index:index + 1, :], empty)
        return jnp.where(is_prev, b_recv[0, index:index + 1, :], other)

    other_peaks = received(1, NEG)
    top = jnp.maximum(peaks, other_peaks)
    keep, add = jnp.exp(peaks - top), jnp.exp(other_peaks - top)
    denom = sums * keep + received(2, 0.0) * add
    denom = jnp.where(denom > 0.0, denom, 1.0)
    attended = ((partial_out * keep + received(0, 0.0) * add) / denom).astype(BF)
    attended2 = heads(attended).astype(F32)
    factor = keep / denom
    factor2 = jnp.concatenate([factor[:, 0:1], factor[:, HEAD:HEAD + 1]], axis=0)
    weights = expo * factor2
    other_factor = add / denom
    base = jnp.where(odd == 0, 0, rows_dev - owned)
    wanted = base + jnp.where(is_prev, -1, slot)
    row = lax.broadcasted_iota(jnp.int32, (slots, rows_dev + window + 16), 1)
    place = jnp.where(row < rows_dev, row, row - odd * (rows_dev + window))
    place = jnp.where(row < rows_dev + window, place, row - (rows_dev + window + 16) - odd * (2 * byte_dev))
    select = jnp.where((place == wanted) & (used | is_prev), 1.0, 0.0).astype(BF)

    def stack(i, value):
        count = width // block
        stack_ref[pl.ds(i * count, count)] = value.astype(BF).reshape(count, block, cols)

    loads[6].wait()
    for copy in ag_copies:
        copy.wait()
    mix_ref[...] = dot(select, mix_buf[...]).astype(BF)
    grad_attended = dot(mix_ref[...], wo_ref[...], NT).astype(BF)
    grad2 = heads(grad_attended)
    delta = jnp.sum(grad2.astype(F32) * attended2, axis=1, keepdims=True)
    grad_scores = (weights * (dot(grad2, v_ref[...], NT) - delta)).astype(BF)
    grad_queries = unheads(dot(grad_scores, k_ref[...]))
    delta = unheads(delta)
    nth = lax.broadcasted_iota(jnp.int32, (HEAD, cols), 0)
    for mask, i in ((is_prev, 0), (is_last, 1)):
        row = row_of(mask, grad_attended.astype(F32))
        column0 = jnp.sum(jnp.where(lane == nth, row, 0.0), axis=1, keepdims=True)
        column1 = jnp.sum(jnp.where(lane == nth + HEAD, row, 0.0), axis=1, keepdims=True)
        whole = jnp.sum(jnp.where(head0, column0, column1) * b_recv[i, 8:8 + HEAD, :], axis=0, keepdims=True)
        whole = whole - row_of(mask, delta) * b_recv[i, 3:4, :]
        grad_queries = grad_queries + jnp.where(mask, row_of(mask, other_factor) * whole, 0.0)
    grad_queries = (grad_queries * scale).astype(BF)
    gk_ref[...] = (dot(grad_scores, queries2, TN) * scale).astype(BF)
    gv_ref[...] = dot(weights.astype(BF), grad2, TN).astype(BF)
    stack(1, dot(bytes_t[...], gk_ref[...]))
    stack(2, dot(bytes_t[...], gv_ref[...]))
    stack(3, dot(mix_ref[...], jnp.where(is_prev, jnp.zeros_like(attended), attended), TN))
    stack(0, dot(pooled_t[...], jnp.where(is_prev, jnp.zeros_like(grad_queries), grad_queries)))

    begins = [sum(len(chunk) for chunk in chunks[:c]) * block for c in range(len(chunks) + 1)]
    opposite, above, below = lax.rem(y + 2, NY), lax.rem(y + 1, NY), lax.rem(y + 3, NY)
    y_copies = {}

    def y_send_to(c, i, src, dst, seq):
        y_copies[c, i] = send(src, dst, y_ssem.at[c, i], y_rsem.at[c, i], seq=seq)
        y_copies[c, i].start()

    def halves(c):
        half = (begins[c + 1] - begins[c]) // 2
        return pl.ds(begins[c], half), pl.ds(begins[c] + half, half)

    def y_first(c):
        for i in range(begins[c] // block, begins[c + 1] // block):
            target = lax.rem(z + order[i] + nz, nz) * NY

            def reorder(q, _, i=i, target=target):
                y_send[q, pl.ds(i * block, block), :] = stack_ref[slots_ref[target + q]]
                return 0

            lax.fori_loop(0, NY, reorder, 0)
        one, two = halves(c)
        y_send_to(c, 0, y_send.at[opposite, one], y_far.at[0, one], plus)
        y_send_to(c, 1, y_send.at[opposite, two], y_far.at[1, two], minus)
        y_send_to(c, 2, y_send.at[above, two], y_dir.at[0, two], plus)
        y_send_to(c, 3, y_send.at[below, one], y_dir.at[1, one], minus)

    def y_second(c):
        one, two = halves(c)
        for i, (rows, q, seq) in enumerate([(one, above, plus), (two, below, minus)]):
            y_copies[c, i].wait_recv()
            value = y_send[q, rows, :].astype(F32) + y_far[i, rows, :].astype(F32)
            y_send[q, rows, :] = value.astype(BF)
            y_send_to(c, 4 + i, y_send.at[q, rows], y_dir.at[i, rows], seq)

    z_copies, far_copies = {}, {}

    def z_rows(o):
        return pl.ds(order.index(o) * block, block)

    def y_sum(c):
        for i in (2, 3, 4, 5):
            y_copies[c, i].wait_recv()
        rows = pl.ds(begins[c], begins[c + 1] - begins[c])
        value = y_send[y, rows, :].astype(F32) + y_dir[0, rows, :].astype(F32) + y_dir[1, rows, :].astype(F32)
        z_send[rows, :] = value.astype(BF)
        for o in chunks[c]:
            if abs(o) > reach:
                i = far.index(o)
                step = o - reach if o > 0 else o + reach
                far_copies[o] = send(
                    z_send.at[z_rows(o)], zf_recv.at[i], zf_ssem.at[i], zf_rsem.at[i], seq=z_peer(step),
                )
                far_copies[o].start()
        for o in sorted((o for o in chunks[c] if 0 < abs(o) <= reach), key=abs):
            if abs(o) == reach:
                value = z_send[z_rows(o), :].astype(F32)
                for i, source in enumerate(far):
                    if (source > 0) == (o > 0):
                        far_copies[source].wait_recv()
                        value = value + zf_recv[i].astype(F32)
                z_send[z_rows(o), :] = value.astype(BF)
            i = near.index(o)
            z_copies[o] = send(z_send.at[z_rows(o)], z_recv.at[i], z_ssem.at[i], z_rsem.at[i], seq=z_peer(o))
            z_copies[o].start()

    p_copies, px_copies = {}, {}

    def p_block(o):
        columns = pl.ds(pl.multiple_of(lax.rem(x + o, nx) * 2 * cols, 2 * cols), 2 * cols)
        value = dot(gk_ref[...], wk_ref[columns, :], NT) + dot(gv_ref[...], wv_ref[columns, :], NT)
        part[o] = (value + dot(mt_ref[...], pb_ref[:, columns])).astype(BF)
        p_copies[o] = send(
            part.at[o, :, mate_half], mate_recv.at[o], p_ssem.at[o], p_rsem.at[o], tp=tp_peer(0, 1),
        )
        p_copies[o].start()

    def p_pair(o):
        p_copies[o].wait_recv()
        return part[o, :, my_half].astype(F32) + mate_recv[o].astype(F32)

    def p_x(o):
        px_send[o - 1] = p_pair(o).astype(BF)
        px_copies[o] = send(
            px_send.at[o - 1], px_recv.at[o - 1], px_ssem.at[o - 1], px_rsem.at[o - 1], tp=tp_peer(o, 0),
        )
        px_copies[o].start()

    y_first(0)
    y_first(1)
    pb_ref[...] = (dot(grad_queries, wq_ref[...], NT) / counts).astype(BF)
    for step in range(max(nx, len(chunks)) + 1):
        if step < nx:
            p_block(x_order(nx)[step])
        if 0 <= step - 2 < len(chunks):
            y_sum(step - 2)
        if step < len(chunks):
            y_second(step)
        if step + 2 < len(chunks):
            y_first(step + 2)
        if 0 < step < nx:
            p_x(x_order(nx)[step - 1])
    for c in range(max(nx, len(chunks)) - 1, len(chunks)):
        y_sum(c)

    mix_mean = (mix_ref[:, mine].astype(F32) / counts).astype(BF)
    total = p_pair(0) + dot(mt_ref[...], mix_mean)
    for o in px_copies:
        px_copies[o].wait_recv()
        total = total + px_recv[o - 1].astype(F32)
    byte_out[...] = total.astype(BF)

    total = z_send[z_rows(0), :].astype(F32)
    for i, o in enumerate(near):
        z_copies[o].wait_recv()
        total = total + z_recv[i].astype(F32)
    owned_out[...] = total
    for copies in (p_copies, px_copies, y_copies, far_copies, z_copies):
        for copy in copies.values():
            copy.wait_send()


def local(
    byte_states, patch_starts, query_weight, key_weight, value_weight, out_weight, up_weight, patch_grad,
    owner_slots, *, n_seq, ntp,
):
    byte_dev, width = byte_states.shape
    pcap = patch_starts.shape[0]
    rows_dev, features = patch_grad.shape
    cols = query_weight.shape[1]
    slots = up16(pcap + 1)
    window = up16(pcap - rows_dev + 1)
    nz, nx = n_seq // NY, ntp // 2
    order = [o for chunk in z_chunks(nz) for o in chunk]
    near = sum(0 < abs(o) <= nz // 4 for o in order)
    far = nz - 1 - near
    block = 4 * width // n_seq
    vmem = pl.BlockSpec(memory_space=pltpu.VMEM)
    hbm = pl.BlockSpec(memory_space=pltpu.HBM)
    dma = pltpu.SemaphoreType.DMA
    return pl.pallas_call(
        functools.partial(kernel, (n_seq, ntp, pcap, rows_dev, window)),
        out_shape=(
            jax.ShapeDtypeStruct((byte_dev, cols), BF),
            jax.ShapeDtypeStruct((block, cols), F32),
        ),
        in_specs=[vmem, pl.BlockSpec(memory_space=pltpu.SMEM)] + [hbm] * 7,
        out_specs=(vmem, vmem),
        scratch_shapes=[
            pltpu.VMEM((byte_dev, width), BF),
            pltpu.VMEM((width, cols), BF),
            pltpu.VMEM((width, cols), BF),
            pltpu.VMEM((width, cols), BF),
            pltpu.VMEM((cols, width), BF),
            pltpu.VMEM((width, features), BF),
            pltpu.VMEM((rows_dev, features), BF),
            pltpu.VMEM((width, byte_dev), BF),
            pltpu.VMEM((byte_dev, cols), BF),
            pltpu.VMEM((byte_dev, cols), BF),
            pltpu.VMEM((byte_dev, cols), BF),
            pltpu.VMEM((byte_dev, cols), BF),
            pltpu.VMEM((slots, width), BF),
            pltpu.VMEM((width, slots), BF),
            pltpu.VMEM((byte_dev, slots), BF),
            pltpu.VMEM((slots, width), BF),
            pltpu.VMEM((slots, width), BF),
            pltpu.VMEM((n_seq, block, cols), BF),
            pltpu.VMEM((rows_dev, 2 * cols), F32),
            pltpu.VMEM((nx, rows_dev, 2 * cols), BF),
            pltpu.VMEM((ntp - 1, rows_dev, cols), BF),
            pltpu.VMEM((rows_dev, cols), BF),
            pltpu.VMEM((rows_dev + window + 16, width), BF),
            pltpu.VMEM((2, 8, width), F32),
            pltpu.VMEM((2, 8, width), F32),
            pltpu.VMEM((2, 8 + HEAD, cols), F32),
            pltpu.VMEM((2, 8 + HEAD, cols), F32),
            pltpu.VMEM((nx, byte_dev, 2 * cols), BF),
            pltpu.VMEM((nx, byte_dev, cols), BF),
            pltpu.VMEM((nx - 1, byte_dev, cols), BF),
            pltpu.VMEM((nx - 1, byte_dev, cols), BF),
            pltpu.VMEM((NY, nz * block, cols), BF),
            pltpu.VMEM((2, nz * block, cols), BF),
            pltpu.VMEM((2, nz * block, cols), BF),
            pltpu.VMEM((nz * block, cols), BF),
            pltpu.VMEM((far, block, cols), BF),
            pltpu.VMEM((near, block, cols), BF),
            dma((7,)),
            dma((ntp - 1,)), dma((ntp - 1,)),
            dma((3, ntp)), dma((3, ntp)),
            dma((2,)), dma((2,)),
            dma((2,)), dma((2,)),
            dma((nx,)), dma((nx,)),
            dma((nx - 1,)), dma((nx - 1,)),
            dma((4, 6)), dma((4, 6)),
            dma((far,)), dma((far,)),
            dma((near,)), dma((near,)),
        ],
        compiler_params=pltpu.CompilerParams(
            collective_id=0, has_side_effects=True, vmem_limit_bytes=62 * 1024 * 1024
        ),
    )(
        patch_starts.reshape(1, pcap), owner_slots, byte_states, query_weight, key_weight, value_weight,
        out_weight, up_weight, patch_grad,
    )


def solution(mesh):
    in_specs = (
        P("seq", None),
        P("seq"),
        P(None, "tp"),
        P(None, "tp"),
        P(None, "tp"),
        P("tp", None),
        P(None, "tp"),
        P("seq", "tp"),
        P(),
    )
    out_specs = (P("seq", "tp"), P("seq", "tp"))
    step = functools.partial(local, n_seq=mesh.shape["seq"], ntp=mesh.shape["tp"])
    return jax.shard_map(step, mesh=mesh, in_specs=in_specs, out_specs=out_specs, check_vma=False)
```

time: 59.7 us -> 51.4 us (0.86)
  the two profiles are of different devices: /device:TPU:1 before, /device:TPU:6 now
where the time goes in v3:
time: 51.4 us; the launch traced here: 51.2 us
  Pallas kernels  47.6 us (93%)
  local copies, waits for them, and re-layouts  2.97 us (6%)
  between operations  0.64 us (1%)
    pallas_call x1, Pallas kernels, local(): pl.pallas_call(functools.partial(kernel, (n_seq, ntp, pcap, rows_dev, win...  47.6 us
    unnamed x2, local copies, waits for them, and re-layouts  2.97 us

profile of v3, /device:TPU:6, one launch (start us, length us, event | category | flops | bytes accessed | tf_op | source)
XLA Modules:
  0.0 51.2 jit_solution(2715094533470537531)
XLA Ops:
  0.6 47.6 %shard_map.104 = (bf16[640,128]{1,0:T(8,128)(2,1)}, f32[64,128]{1,0:T(8,128)}) custom-call(s32[1,140]{1,0:T(1,128)} %bitcast.1, s32[64]{0:T(128)} %slots_ref.1, bf16[640,1024]{1,0:T(8,128)(2,1)} %bytes_hbm.1, bf16[1024,128]{1,0:T(8,128)(2,1)} %wq_hbm.1, bf16[1024,128]{1,0:T(8,128)(2,1)} %wk_hbm.1, bf16[1024,128]{1,0:T(8,128)(2,1)} %wv_hbm.1, ...), custom_call_target="tpu_custom_call" | custom-call | tf_op jit(solution)/shard_map/pallas_call | solution.py:438
  48.2 1.6 %copy.13 = bf16[640,128]{1,0:T(8,128)(2,1)} copy(bf16[640,128]{1,0:T(8,128)(2,1)} %get-tuple-element.4) | data formatting | bytes 327680
  49.8 1.4 %copy.14 = f32[64,128]{1,0:T(8,128)} copy(f32[64,128]{1,0:T(8,128)} %get-tuple-element.5) | data formatting | bytes 65536

commit v4 on v3

--- a/solution.py
+++ b/solution.py
@@ -48,9 +48,9 @@
 
 def kernel(
     sizes,
-    starts_ref, slots_ref, bytes_hbm, wq_hbm, wk_hbm, wv_hbm, wo_hbm, up_hbm, pg_hbm,
+    starts_hbm, slots_hbm, bytes_hbm, wq_hbm, wk_hbm, wv_hbm, wo_hbm, up_hbm, pg_hbm,
     byte_out, owned_out,
-    bytes_ref, wq_ref, wk_ref, wv_ref, wo_ref, up_ref, pg_ref,
+    starts_ref, slots_ref, bytes_ref, wq_ref, wk_ref, wv_ref, wo_ref, up_ref, pg_ref,
     bytes_t, k_ref, v_ref, gk_ref, gv_ref, pooled_ref, pooled_t, mt_ref, mix_ref, pb_ref, stack_ref,
     gm_first, gm_send, gm_recv, mix_own, mix_buf,
     a_send, a_recv, b_send, b_recv,
@@ -100,7 +100,7 @@
         pltpu.make_async_copy(src, dst, load_sem.at[i])
         for i, (src, dst) in enumerate([
             (pg_hbm, pg_ref), (up_hbm, up_ref), (bytes_hbm, bytes_ref), (wk_hbm, wk_ref),
-            (wv_hbm, wv_ref), (wq_hbm, wq_ref), (wo_hbm, wo_ref),
+            (wv_hbm, wv_ref), (wq_hbm, wq_ref), (wo_hbm, wo_ref), (starts_hbm, starts_ref), (slots_hbm, slots_ref),
         ])
     ]
     for load in loads:
@@ -130,6 +130,7 @@
         gm_copies.append(send(gm_send.at[o, :, half], gm_recv.at[k], gm_ssem.at[k], gm_rsem.at[k], tp=tp_peer(o, d)))
         gm_copies[-1].start()
 
+    loads[7].wait()
     starts = starts_ref[...].astype(F32)
     slot = lax.broadcasted_iota(jnp.int32, (slots, 1), 0)
     nth = lax.broadcasted_iota(jnp.int32, (slots, pcap), 1)
@@ -383,6 +384,7 @@
         )
         px_copies[o].start()
 
+    loads[8].wait()
     y_first(0)
     y_first(1)
     pb_ref[...] = (dot(grad_queries, wq_ref[...], NT) / counts).astype(BF)
@@ -441,9 +443,11 @@
             jax.ShapeDtypeStruct((byte_dev, cols), BF),
             jax.ShapeDtypeStruct((block, cols), F32),
         ),
-        in_specs=[vmem, pl.BlockSpec(memory_space=pltpu.SMEM)] + [hbm] * 7,
+        in_specs=[hbm] * 9,
         out_specs=(vmem, vmem),
         scratch_shapes=[
+            pltpu.VMEM((1, pcap), jnp.int32),
+            pltpu.SMEM((n_seq,), jnp.int32),
             pltpu.VMEM((byte_dev, width), BF),
             pltpu.VMEM((width, cols), BF),
             pltpu.VMEM((width, cols), BF),
@@ -481,7 +485,7 @@
             pltpu.VMEM((nz * block, cols), BF),
             pltpu.VMEM((far, block, cols), BF),
             pltpu.VMEM((near, block, cols), BF),
-            dma((7,)),
+            dma((9,)),
             dma((ntp - 1,)), dma((ntp - 1,)),
             dma((3, ntp)), dma((3, ntp)),
             dma((2,)), dma((2,)),
@@ -493,12 +497,15 @@
             dma((near,)), dma((near,)),
         ],
         compiler_params=pltpu.CompilerParams(
-            collective_id=0, has_side_effects=True, vmem_limit_bytes=62 * 1024 * 1024
+            collective_id=0, has_side_effects=True, vmem_limit_bytes=40 * 1024 * 1024
         ),
-    )(
-        patch_starts.reshape(1, pcap), owner_slots, byte_states, query_weight, key_weight, value_weight,
-        out_weight, up_weight, patch_grad,
-    )
+    )(*[
+        pltpu.with_memory_space_constraint(operand, pltpu.HBM)
+        for operand in (
+            patch_starts.reshape(1, pcap), owner_slots, byte_states, query_weight, key_weight, value_weight,
+            out_weight, up_weight, patch_grad,
+        )
+    ])
 
 
 def solution(mesh):

time: 51.4 us -> 48.4 us (0.942)
  Pallas kernels: 47.6 us -> 45.9 us
  local copies, waits for them, and re-layouts: 2.97 us -> 1.28 us
    unnamed x2, local copies, waits for them, and re-layouts: 2.97 us -> 1.28 us
    pallas_call x1, Pallas kernels: 47.6 us -> 45.9 us  [local(): pl.pallas_call(functools.partial(kernel, (n_seq, ntp, pcap, rows_dev, win...]
where the time goes in v4:
time: 48.4 us; the launch traced here: 47.8 us
  Pallas kernels  45.9 us (95%)
  local copies, waits for them, and re-layouts  1.28 us (3%)
  between operations  0.64 us (1%)
    pallas_call x1, Pallas kernels, local(): pl.pallas_call(functools.partial(kernel, (n_seq, ntp, pcap, rows_dev, win...  45.9 us
    unnamed x2, local copies, waits for them, and re-layouts  1.28 us

profile of v4, /device:TPU:6, one launch (start us, length us, event | category | flops | bytes accessed | tf_op | source)
XLA Modules:
  0.0 47.8 jit_solution(6884616310001649676)
XLA Ops:
  0.6 45.9 %shard_map.104 = (bf16[640,128]{1,0:T(8,128)(2,1)S(1)}, f32[64,128]{1,0:T(8,128)S(1)}) custom-call(s32[1,140]{1,0:T(1,128)} %bitcast.1, s32[64]{0:T(128)} %slots_hbm.1, bf16[640,1024]{1,0:T(8,128)(2,1)} %bytes_hbm.1, bf16[1024,128]{1,0:T(8,128)(2,1)} %wq_hbm.1, bf16[1024,128]{1,0:T(8,128)(2,1)} %wk_hbm.1, bf16[1024,128]{1,0:T(8,128)(2,1)} %wv_hbm.1, ...), custom_call_target="tpu_custom_call" | custom-call | tf_op jit(solution)/shard_map/pallas_call | solution.py:440
  46.5 0.7 %copy.13 = bf16[640,128]{1,0:T(8,128)(2,1)} copy(bf16[640,128]{1,0:T(8,128)(2,1)S(1)} %get-tuple-element.4) | data formatting | bytes 327680
  47.2 0.6 %copy.14 = f32[64,128]{1,0:T(8,128)} copy(f32[64,128]{1,0:T(8,128)S(1)} %get-tuple-element.5) | data formatting | bytes 65536

commit v5 on v4

--- a/solution.py
+++ b/solution.py
@@ -387,20 +387,24 @@
     loads[8].wait()
     y_first(0)
     y_first(1)
+    y_first(2)
     pb_ref[...] = (dot(grad_queries, wq_ref[...], NT) / counts).astype(BF)
-    for step in range(max(nx, len(chunks)) + 1):
-        if step < nx:
-            p_block(x_order(nx)[step])
-        if 0 <= step - 2 < len(chunks):
-            y_sum(step - 2)
-        if step < len(chunks):
-            y_second(step)
-        if step + 2 < len(chunks):
-            y_first(step + 2)
-        if 0 < step < nx:
-            p_x(x_order(nx)[step - 1])
-    for c in range(max(nx, len(chunks)) - 1, len(chunks)):
-        y_sum(c)
+    y_second(0)
+    p_block(2)
+    y_second(1)
+    y_first(3)
+    p_block(1)
+    y_sum(0)
+    y_second(2)
+    p_x(2)
+    p_block(3)
+    y_sum(1)
+    y_second(3)
+    p_x(1)
+    p_block(0)
+    p_x(3)
+    y_sum(2)
+    y_sum(3)
 
     mix_mean = (mix_ref[:, mine].astype(F32) / counts).astype(BF)
     total = p_pair(0) + dot(mt_ref[...], mix_mean)

time: 48.4 us -> 48.1 us (level)
  no operation moved by 1% of the time
where the time goes in v5:
time: 48.1 us; the launch traced here: 48 us
  Pallas kernels  46 us (96%)
  local copies, waits for them, and re-layouts  1.28 us (3%)
  between operations  0.64 us (1%)
    pallas_call x1, Pallas kernels, local(): pl.pallas_call(functools.partial(kernel, (n_seq, ntp, pcap, rows_dev, win...  46 us
    unnamed x2, local copies, waits for them, and re-layouts  1.28 us

profile of v5, /device:TPU:6, one launch (start us, length us, event | category | flops | bytes accessed | tf_op | source)
XLA Modules:
  0.0 48.0 jit_solution(5786023067293319883)
XLA Ops:
  0.6 46.0 %shard_map.104 = (bf16[640,128]{1,0:T(8,128)(2,1)S(1)}, f32[64,128]{1,0:T(8,128)S(1)}) custom-call(s32[1,140]{1,0:T(1,128)} %bitcast.1, s32[64]{0:T(128)} %slots_hbm.1, bf16[640,1024]{1,0:T(8,128)(2,1)} %bytes_hbm.1, bf16[1024,128]{1,0:T(8,128)(2,1)} %wq_hbm.1, bf16[1024,128]{1,0:T(8,128)(2,1)} %wk_hbm.1, bf16[1024,128]{1,0:T(8,128)(2,1)} %wv_hbm.1, ...), custom_call_target="tpu_custom_call" | custom-call | tf_op jit(solution)/shard_map/pallas_call | solution.py:444
  46.7 0.7 %copy.13 = bf16[640,128]{1,0:T(8,128)(2,1)} copy(bf16[640,128]{1,0:T(8,128)(2,1)S(1)} %get-tuple-element.4) | data formatting | bytes 327680
  47.4 0.6 %copy.14 = f32[64,128]{1,0:T(8,128)} copy(f32[64,128]{1,0:T(8,128)S(1)} %get-tuple-element.5) | data formatting | bytes 65536

commit v6 on v5

--- a/solution.py
+++ b/solution.py
@@ -103,17 +103,17 @@
             (wv_hbm, wv_ref), (wq_hbm, wq_ref), (wo_hbm, wo_ref), (starts_hbm, starts_ref), (slots_hbm, slots_ref),
         ])
     ]
-    for load in loads:
-        load.start()
-
     barrier = pltpu.get_barrier_semaphore()
     peers = [{"tp": tp_peer(o, d)} for o, d in others]
     peers += [{"seq": partner, "tp": tp_peer(o, d)} for o, d in everyone]
     peers += [{"seq": before, "tp": tp_peer(o, d)} for o, d in everyone]
     peers += [{"seq": following}, {"seq": plus}, {"seq": minus}]
     peers += [{"seq": z_peer(o)} for o in near]
-    for peer in peers:
+    for peer in reversed(peers):
         pl.semaphore_signal(barrier, inc=1, device_id=peer, device_id_type=pl.DeviceIdType.MESH)
+
+    for load in loads:
+        load.start()
 
     loads[0].wait()
     loads[1].wait()

time: 48.1 us -> 48.5 us (level)
  no operation moved by 1% of the time
where the time goes in v6:
time: 48.5 us; the launch traced here: 48.1 us
  Pallas kernels  46.1 us (95%)
  local copies, waits for them, and re-layouts  1.28 us (3%)
  between operations  0.64 us (1%)
    pallas_call x1, Pallas kernels, local(): pl.pallas_call(functools.partial(kernel, (n_seq, ntp, pcap, rows_dev, win...  46.1 us
    unnamed x2, local copies, waits for them, and re-layouts  1.28 us

profile of v6, /device:TPU:6, one launch (start us, length us, event | category | flops | bytes accessed | tf_op | source)
XLA Modules:
  0.0 48.1 jit_solution(3433652949931739671)
XLA Ops:
  0.6 46.1 %shard_map.104 = (bf16[640,128]{1,0:T(8,128)(2,1)S(1)}, f32[64,128]{1,0:T(8,128)S(1)}) custom-call(s32[1,140]{1,0:T(1,128)} %bitcast.1, s32[64]{0:T(128)} %slots_hbm.1, bf16[640,1024]{1,0:T(8,128)(2,1)} %bytes_hbm.1, bf16[1024,128]{1,0:T(8,128)(2,1)} %wq_hbm.1, bf16[1024,128]{1,0:T(8,128)(2,1)} %wk_hbm.1, bf16[1024,128]{1,0:T(8,128)(2,1)} %wv_hbm.1, ...), custom_call_target="tpu_custom_call" | custom-call | tf_op jit(solution)/shard_map/pallas_call | solution.py:444
  46.8 0.7 %copy.13 = bf16[640,128]{1,0:T(8,128)(2,1)} copy(bf16[640,128]{1,0:T(8,128)(2,1)S(1)} %get-tuple-element.4) | data formatting | bytes 327680
  47.5 0.6 %copy.14 = f32[64,128]{1,0:T(8,128)} copy(f32[64,128]{1,0:T(8,128)S(1)} %get-tuple-element.5) | data formatting | bytes 65536
